TPU v7x, 256 devices: a whole 4x4x8 slice. The times are simulated.
256 devices in a mesh: inst: 16 (over z, x_hi), head: 16 (over x_lo, y, core).
Axes of the slice: x: 4 (x_hi: 2, x_lo: 2; x = x_hi * 2 + x_lo), y: 4, z: 8, core: 2. Of those that a mesh axis runs over, the one named last changes fastest.
Arguments:
- queries: bfloat16 [16, 128, 128], P('inst', 'head'), may hold values from -6 to 6
- page_pool: bfloat16 [4352, 2, 16, 64, 128], P('inst', None, 'head'), may hold values from -6 to 6, as said below
- block_tables: int32 [16, 16, 16], P(None, 'inst'), may hold values from 0 to 271, as said below
- token_counts: int32 [16, 16], P(None, 'inst'), may hold values from 1 to 1024, as said below
- move_slots: int32 [16, 32], P('inst'), may hold values from 0 to 271, as said below
- out_weight: bfloat16 [16384, 16384], P('head', 'inst'), may hold values from -0.046875 to 0.046875
Outputs:
- projected: bfloat16 [16, 16384], P('head', 'inst')
- arrived: bfloat16 [512, 2, 16, 64, 128], P('inst', None, 'head')
Inputs may be any that keep to these rules, and one draw needn't show every extreme that they name: `block_tables`: in each instance the slots of all requests and pages are distinct. `token_counts`: every request has 1024 tokens on some instance. `move_slots`: distinct within each instance. `page_pool`: stored heads c and c2 are equal wherever c * 8 // 16 == c2 * 8 // 16: copies of one key-value head of the model.
All inputs are finite; a program needn't handle non-finite values.
Results may differ from a plain program's by a relative error of at most 0.007.
Values may be sent and summed in bfloat16 or wider, within the bound.
No kernel may reach another device: no remote copies, remote signals or barrier semaphores. Data moves between devices by JAX's collectives and lax.ppermute only.
A program may use at most 128 MiB of HBM per device.

v0:
```python
import jax
import jax.numpy as jnp
from jax import lax
from jax.sharding import PartitionSpec as P

NEG_BIG = -1e30


def passed_along(block, axis, distance):
    devices = range(lax.axis_size(axis))
    route = [((i - distance) % len(devices), i) for i in devices]
    return lax.ppermute(block, axis, route)


def local_partial(query_tile, owner_idx, page_pool, block_tables, token_counts):
    rows = query_tile.shape[0]
    head_count = query_tile.shape[1]
    head_size = query_tile.shape[2]
    kv_count = page_pool.shape[2]
    page_len = page_pool.shape[3]
    group = head_count // kv_count
    page_slots = lax.dynamic_slice_in_dim(block_tables, owner_idx * rows, rows, 0)[:, 0, :]
    live_counts = lax.dynamic_slice_in_dim(token_counts, owner_idx * rows, rows, 0)[:, 0]
    pages = jnp.take(page_pool, page_slots, axis=0)
    page_keys = pages[:, :, 0]
    page_values = pages[:, :, 1]
    query_rows = query_tile.reshape(rows, kv_count, group, head_size)
    scores = jnp.einsum(
        "rcgd,rpctd->rcgpt", query_rows, page_keys, preferred_element_type=jnp.float32
    )
    scores = scores * (1.0 / head_size**0.5)
    positions = (
        jnp.arange(page_slots.shape[1], dtype=jnp.int32)[:, None] * page_len
        + jnp.arange(page_len, dtype=jnp.int32)[None, :]
    )
    token_live = positions[None, :, :] < live_counts[:, None, None]
    masked = jnp.where(token_live[:, None, None], scores, NEG_BIG)
    best_max = jnp.max(masked, axis=(3, 4))
    weights = jnp.exp(masked - best_max[..., None, None]).astype(jnp.bfloat16)
    weight_sum = jnp.sum(weights.astype(jnp.float32), axis=(3, 4))
    accum_out = jnp.einsum(
        "rcgpt,rpctd->rcgd", weights, page_values, preferred_element_type=jnp.float32
    )
    return (
        best_max.reshape(rows, head_count),
        weight_sum.reshape(rows, head_count),
        accum_out.reshape(rows, head_count, head_size),
    )


def combine_parts(first, second):
    top = jnp.maximum(first[0], second[0])
    scale_one = jnp.exp(first[0] - top)
    scale_two = jnp.exp(second[0] - top)
    total = first[1] * scale_one + second[1] * scale_two
    output = first[2] * scale_one[..., None] + second[2] * scale_two[..., None]
    return (top, total, output)


def body(queries, page_pool, block_tables, token_counts, move_slots, out_weight):
    inst_count = lax.axis_size("inst")
    inst_here = lax.axis_index("inst")
    outgoing = jnp.take(page_pool, move_slots[0], axis=0)
    arrived = passed_along(outgoing, "inst", inst_count // 2)
    rows = queries.shape[0]
    head_count = queries.shape[1]
    head_size = queries.shape[2]
    start_state = (
        queries.astype(jnp.float32),
        jnp.full((rows, head_count), NEG_BIG, jnp.float32),
        jnp.zeros((rows, head_count), jnp.float32),
        jnp.zeros((rows, head_count, head_size), jnp.float32),
    )

    def visit_step(step_idx, carry):
        query_tile, best_max, weight_sum, accum_out = carry
        owner_idx = (inst_here - step_idx) % inst_count
        part = local_partial(
            query_tile.astype(jnp.bfloat16), owner_idx, page_pool, block_tables, token_counts
        )
        best_max, weight_sum, accum_out = combine_parts((best_max, weight_sum, accum_out), part)
        return passed_along((query_tile, best_max, weight_sum, accum_out), "inst", 1)

    final_state = lax.fori_loop(0, inst_count, visit_step, start_state)
    attended = (final_state[3] / final_state[2][..., None]).astype(jnp.bfloat16)
    piece = lax.all_gather(attended, "inst", axis=0, tiled=True)
    terms = jnp.dot(
        piece.reshape(piece.shape[0], head_count * head_size),
        out_weight,
        preferred_element_type=jnp.float32,
    )
    projected = lax.psum_scatter(terms, "head", scatter_dimension=0, tiled=True).astype(
        jnp.bfloat16
    )
    return (projected, arrived)


def solution(mesh):
    in_specs = (
        P("inst", "head", None),
        P("inst", None, "head", None, None),
        P(None, "inst", None),
        P(None, "inst"),
        P("inst", None),
        P("head", "inst"),
    )
    out_specs = (P("head", "inst"), P("inst", None, "head", None, None))
    return jax.shard_map(body, mesh=mesh, in_specs=in_specs, out_specs=out_specs, check_vma=False)
```

profile of v0, /device:TPU:1, one launch (start us, length us, event | category | flops | bytes accessed | tf_op | source)
XLA Modules:
  0.0 450.1 jit_solution(2375058747608950370)
XLA Ops:
  2.2 4.3 gather_fusion.1
  7.6 7.7 %collective-permute-start.4 = (bf16[32,2,1,64,128]{4,3,2,1,0:T(8,128)(2,1)}, bf16[32,2,1,64,128]{4,3,2,1,0:T(8,128)(2,1)}, u32[]{:S(2)}, u32[]{:S(2)}) collective-permute-start(bf16[32,2,1,64,128]{4,3,2,1,0:T(8,128)(2,1)} %bitcast_select_fusion.1), channel_id=1, source_target_pairs={{128,0},{144,16},{160,32},{176,48},{192,64},{208,80},{224,96},{240... | collective-permute-start | bytes 3145736 | tf_op jit(solution)/shard_map/ppermute | solution.py:12
  16.0 311.9 %while.21 = (s32[]{:T(128)}, bf16[1,8,128]{2,1,0:T(8,128)(2,1)S(1)}, f32[1,8]{1,0:T(1,128)S(1)}, f32[1,8]{1,0:T(1,128)S(1)}, f32[1,8,128]{2,1,0:T(8,128)S(1)}, /...) while((s32[]{:T(128)}, ...), condition=%wide.region_3.4_spmd, body=%wide.region_0.3_spmd.sunk | while | flops 4536529 | bytes 2801680 | solution.py:84
  18.7 4.2 gather_fusion
  30.8 19.7 %collective-permute-done.1 = f32[1,8]{1,0:T(1,128)S(1)} collective-permute-done((f32[1,8]{1,0:T(1,128)S(1)}, f32[1,8]{1,0:T(1,128)S(1)}, u32[]{:S(2)}, u32[]{:S(2)}) %collective-permute-start.1) | collective-permute-done | bytes 64 | tf_op jit(solution)/shard_map/while/body/eval_jaxpr/ppermute | solution.py:12
  53.3 4.2 gather_fusion
  59.8 5.8 %collective-permute-done.1 = f32[1,8]{1,0:T(1,128)S(1)} collective-permute-done((f32[1,8]{1,0:T(1,128)S(1)}, f32[1,8]{1,0:T(1,128)S(1)}, u32[]{:S(2)}, u32[]{:S(2)}) %collective-permute-start.1) | collective-permute-done | bytes 64 | tf_op jit(solution)/shard_map/while/body/eval_jaxpr/ppermute | solution.py:12
  68.4 4.2 gather_fusion
  73.7 12.5 %collective-permute-start.3 = (f32[1,8,128]{2,1,0:T(8,128)S(1)}, f32[1,8,128]{2,1,0:T(8,128)S(1)}, u32[]{:S(2)}, u32[]{:S(2)}) collective-permute-start(f32[1,8,128]{2,1,0:T(8,128)S(1)} %fusion.28), channel_id=1, source_target_pairs={{240,0},{0,16},{16,32},{32,48},{48,64},{64,80},{80,96},{96,112},{1... | collective-permute-start | bytes 12296 | tf_op jit(solution)/shard_map/while/body/eval_jaxpr/ppermute | solution.py:12
  86.2 4.3 collective-permute-start
  102.4 4.2 gather_fusion
  110.1 4.8 %collective-permute-done.1 = f32[1,8]{1,0:T(1,128)S(1)} collective-permute-done((f32[1,8]{1,0:T(1,128)S(1)}, f32[1,8]{1,0:T(1,128)S(1)}, u32[]{:S(2)}, u32[]{:S(2)}) %collective-permute-start.1) | collective-permute-done | bytes 64 | tf_op jit(solution)/shard_map/while/body/eval_jaxpr/ppermute | solution.py:12
  117.8 4.2 gather_fusion
  123.5 5.3 %collective-permute-start.2 = (f32[1,8]{1,0:T(1,128)S(1)}, f32[1,8]{1,0:T(1,128)S(1)}, u32[]{:S(2)}, u32[]{:S(2)}) collective-permute-start(f32[1,8]{1,0:T(1,128)S(1)} %get-tuple-element.332), channel_id=1, source_target_pairs={{240,0},{0,16},{16,32},{32,48},{48,64},{64,80},{80,96},{96,112},{1... | collective-permute-start | bytes 104 | tf_op jit(solution)/shard_map/while/body/eval_jaxpr/ppermute | solution.py:12
  132.2 4.2 gather_fusion
  145.7 4.9 %collective-permute-done.1 = f32[1,8]{1,0:T(1,128)S(1)} collective-permute-done((f32[1,8]{1,0:T(1,128)S(1)}, f32[1,8]{1,0:T(1,128)S(1)}, u32[]{:S(2)}, u32[]{:S(2)}) %collective-permute-start.1) | collective-permute-done | bytes 64 | tf_op jit(solution)/shard_map/while/body/eval_jaxpr/ppermute | solution.py:12
  153.4 4.2 gather_fusion
  167.7 4.2 gather_fusion
  190.3 4.2 gather_fusion
  200.8 4.9 %collective-permute-done.1 = f32[1,8]{1,0:T(1,128)S(1)} collective-permute-done((f32[1,8]{1,0:T(1,128)S(1)}, f32[1,8]{1,0:T(1,128)S(1)}, u32[]{:S(2)}, u32[]{:S(2)}) %collective-permute-start.1) | collective-permute-done | bytes 64 | tf_op jit(solution)/shard_map/while/body/eval_jaxpr/ppermute | solution.py:12
  208.5 4.2 gather_fusion
  216.4 4.4 collective-permute-done.1
  223.6 4.2 gather_fusion
  242.9 4.2 gather_fusion
  251.6 4.9 %collective-permute-done.1 = f32[1,8]{1,0:T(1,128)S(1)} collective-permute-done((f32[1,8]{1,0:T(1,128)S(1)}, f32[1,8]{1,0:T(1,128)S(1)}, u32[]{:S(2)}, u32[]{:S(2)}) %collective-permute-start.1) | collective-permute-done | bytes 64 | tf_op jit(solution)/shard_map/while/body/eval_jaxpr/ppermute | solution.py:12
  259.3 4.2 gather_fusion
  277.9 4.2 gather_fusion
  298.0 4.2 gather_fusion
  306.6 4.9 %collective-permute-done.1 = f32[1,8]{1,0:T(1,128)S(1)} collective-permute-done((f32[1,8]{1,0:T(1,128)S(1)}, f32[1,8]{1,0:T(1,128)S(1)}, u32[]{:S(2)}, u32[]{:S(2)}) %collective-permute-start.1) | collective-permute-done | bytes 64 | tf_op jit(solution)/shard_map/while/body/eval_jaxpr/ppermute | solution.py:12
  314.6 4.2 gather_fusion
  328.0 31.4 %all_gather.3 = bf16[16,8,128]{2,1,0:T(8,128)(2,1)S(1)} all-gather(bf16[1,8,128]{2,1,0:T(8,128)(2,1)S(1)} %divide_convert_fusion), channel_id=1, replica_groups=mesh['inst'=16,'head'=16] {'inst'}, dimensions={0}, use_global_device_ids=true | all-gather | bytes 34816 | tf_op jit(solution)/shard_map/all_gather | solution.py:86
  359.8 86.8 %all-reduce = bf16[16,1024]{1,0:T(8,128)(2,1)S(1)} all-reduce(f32[16,1024]{1,0:T(8,128)S(1)} %fusion.13), channel_id=2, replica_groups=mesh['inst'=16,'head'=16] {'head'}, use_global_device_ids=true, to_apply=%region_4.5.clone | all-reduce | flops 16384 | bytes 98304
  (330 shorter events, 175.1 us)
Async XLA Ops:
  7.6 440.2 %collective-permute-start.4 = (bf16[32,2,1,64,128]{4,3,2,1,0:T(8,128)(2,1)}, bf16[32,2,1,64,128]{4,3,2,1,0:T(8,128)(2,1)}, u32[]{:S(2)}, u32[]{:S(2)}) collective-permute-start(bf16[32,2,1,64,128]{4,3,2,1,0:T(8,128)(2,1)} %bitcast_select_fusion.1), channel_id=1, source_target_pairs={{128,0},{144,16},{160,32},{176,48},{192,64},{208,80},{224,96},{240... | collective-permute-start | bytes 3145736 | tf_op jit(solution)/shard_map/ppermute | solution.py:12
  24.0 26.6 %collective-permute-start.3 = (f32[1,8,128]{2,1,0:T(8,128)S(1)}, f32[1,8,128]{2,1,0:T(8,128)S(1)}, u32[]{:S(2)}, u32[]{:S(2)}) collective-permute-start(f32[1,8,128]{2,1,0:T(8,128)S(1)} %fusion.28), channel_id=1, source_target_pairs={{240,0},{0,16},{16,32},{32,48},{48,64},{64,80},{80,96},{96,112},{1... | collective-permute-start | bytes 12296 | tf_op jit(solution)/shard_map/while/body/eval_jaxpr/ppermute | solution.py:12
  26.7 23.9 %collective-permute-start = (bf16[1,8,128]{2,1,0:T(8,128)(2,1)S(1)}, bf16[1,8,128]{2,1,0:T(8,128)(2,1)S(1)}, u32[]{:S(2)}, u32[]{:S(2)}) collective-permute-start(bf16[1,8,128]{2,1,0:T(8,128)(2,1)S(1)} %copy.26), channel_id=1, source_target_pairs={{240,0},{0,16},{16,32},{32,48},{48,64},{64,80},{80,96},{96,112},{1... | collective-permute-start | bytes 6152 | tf_op jit(solution)/shard_map/while/body/eval_jaxpr/ppermute | solution.py:12
  27.4 23.2 %collective-permute-start.1 = (f32[1,8]{1,0:T(1,128)S(1)}, f32[1,8]{1,0:T(1,128)S(1)}, u32[]{:S(2)}, u32[]{:S(2)}) collective-permute-start(f32[1,8]{1,0:T(1,128)S(1)} %get-tuple-element.331), channel_id=1, source_target_pairs={{240,0},{0,16},{16,32},{32,48},{48,64},{64,80},{80,96},{96,112},{1... | collective-permute-start | bytes 104 | tf_op jit(solution)/shard_map/while/body/eval_jaxpr/ppermute | solution.py:12
  30.2 20.4 %collective-permute-start.2 = (f32[1,8]{1,0:T(1,128)S(1)}, f32[1,8]{1,0:T(1,128)S(1)}, u32[]{:S(2)}, u32[]{:S(2)}) collective-permute-start(f32[1,8]{1,0:T(1,128)S(1)} %get-tuple-element.332), channel_id=1, source_target_pairs={{240,0},{0,16},{16,32},{32,48},{48,64},{64,80},{80,96},{96,112},{1... | collective-permute-start | bytes 104 | tf_op jit(solution)/shard_map/while/body/eval_jaxpr/ppermute | solution.py:12
  58.6 7.2 %collective-permute-start.3 = (f32[1,8,128]{2,1,0:T(8,128)S(1)}, f32[1,8,128]{2,1,0:T(8,128)S(1)}, u32[]{:S(2)}, u32[]{:S(2)}) collective-permute-start(f32[1,8,128]{2,1,0:T(8,128)S(1)} %fusion.28), channel_id=1, source_target_pairs={{240,0},{0,16},{16,32},{32,48},{48,64},{64,80},{80,96},{96,112},{1... | collective-permute-start | bytes 12296 | tf_op jit(solution)/shard_map/while/body/eval_jaxpr/ppermute | solution.py:12
  58.6 7.2 %collective-permute-start = (bf16[1,8,128]{2,1,0:T(8,128)(2,1)S(1)}, bf16[1,8,128]{2,1,0:T(8,128)(2,1)S(1)}, u32[]{:S(2)}, u32[]{:S(2)}) collective-permute-start(bf16[1,8,128]{2,1,0:T(8,128)(2,1)S(1)} %copy.26), channel_id=1, source_target_pairs={{240,0},{0,16},{16,32},{32,48},{48,64},{64,80},{80,96},{96,112},{1... | collective-permute-start | bytes 6152 | tf_op jit(solution)/shard_map/while/body/eval_jaxpr/ppermute | solution.py:12
  73.7 26.0 %collective-permute-start.3 = (f32[1,8,128]{2,1,0:T(8,128)S(1)}, f32[1,8,128]{2,1,0:T(8,128)S(1)}, u32[]{:S(2)}, u32[]{:S(2)}) collective-permute-start(f32[1,8,128]{2,1,0:T(8,128)S(1)} %fusion.28), channel_id=1, source_target_pairs={{240,0},{0,16},{16,32},{32,48},{48,64},{64,80},{80,96},{96,112},{1... | collective-permute-start | bytes 12296 | tf_op jit(solution)/shard_map/while/body/eval_jaxpr/ppermute | solution.py:12
  86.2 13.5 %collective-permute-start = (bf16[1,8,128]{2,1,0:T(8,128)(2,1)S(1)}, bf16[1,8,128]{2,1,0:T(8,128)(2,1)S(1)}, u32[]{:S(2)}, u32[]{:S(2)}) collective-permute-start(bf16[1,8,128]{2,1,0:T(8,128)(2,1)S(1)} %copy.26), channel_id=1, source_target_pairs={{240,0},{0,16},{16,32},{32,48},{48,64},{64,80},{80,96},{96,112},{1... | collective-permute-start | bytes 6152 | tf_op jit(solution)/shard_map/while/body/eval_jaxpr/ppermute | solution.py:12
  107.6 7.5 %collective-permute-start.3 = (f32[1,8,128]{2,1,0:T(8,128)S(1)}, f32[1,8,128]{2,1,0:T(8,128)S(1)}, u32[]{:S(2)}, u32[]{:S(2)}) collective-permute-start(f32[1,8,128]{2,1,0:T(8,128)S(1)} %fusion.28), channel_id=1, source_target_pairs={{240,0},{0,16},{16,32},{32,48},{48,64},{64,80},{80,96},{96,112},{1... | collective-permute-start | bytes 12296 | tf_op jit(solution)/shard_map/while/body/eval_jaxpr/ppermute | solution.py:12
  107.7 7.4 %collective-permute-start = (bf16[1,8,128]{2,1,0:T(8,128)(2,1)S(1)}, bf16[1,8,128]{2,1,0:T(8,128)(2,1)S(1)}, u32[]{:S(2)}, u32[]{:S(2)}) collective-permute-start(bf16[1,8,128]{2,1,0:T(8,128)(2,1)S(1)} %copy.26), channel_id=1, source_target_pairs={{240,0},{0,16},{16,32},{32,48},{48,64},{64,80},{80,96},{96,112},{1... | collective-permute-start | bytes 6152 | tf_op jit(solution)/shard_map/while/body/eval_jaxpr/ppermute | solution.py:12
  137.4 13.4 %collective-permute-start.3 = (f32[1,8,128]{2,1,0:T(8,128)S(1)}, f32[1,8,128]{2,1,0:T(8,128)S(1)}, u32[]{:S(2)}, u32[]{:S(2)}) collective-permute-start(f32[1,8,128]{2,1,0:T(8,128)S(1)} %fusion.28), channel_id=1, source_target_pairs={{240,0},{0,16},{16,32},{32,48},{48,64},{64,80},{80,96},{96,112},{1... | collective-permute-start | bytes 12296 | tf_op jit(solution)/shard_map/while/body/eval_jaxpr/ppermute | solution.py:12
  140.6 10.2 %collective-permute-start = (bf16[1,8,128]{2,1,0:T(8,128)(2,1)S(1)}, bf16[1,8,128]{2,1,0:T(8,128)(2,1)S(1)}, u32[]{:S(2)}, u32[]{:S(2)}) collective-permute-start(bf16[1,8,128]{2,1,0:T(8,128)(2,1)S(1)} %copy.26), channel_id=1, source_target_pairs={{240,0},{0,16},{16,32},{32,48},{48,64},{64,80},{80,96},{96,112},{1... | collective-permute-start | bytes 6152 | tf_op jit(solution)/shard_map/while/body/eval_jaxpr/ppermute | solution.py:12
  173.0 14.6 %collective-permute-start.3 = (f32[1,8,128]{2,1,0:T(8,128)S(1)}, f32[1,8,128]{2,1,0:T(8,128)S(1)}, u32[]{:S(2)}, u32[]{:S(2)}) collective-permute-start(f32[1,8,128]{2,1,0:T(8,128)S(1)} %fusion.28), channel_id=1, source_target_pairs={{240,0},{0,16},{16,32},{32,48},{48,64},{64,80},{80,96},{96,112},{1... | collective-permute-start | bytes 12296 | tf_op jit(solution)/shard_map/while/body/eval_jaxpr/ppermute | solution.py:12
  174.3 13.3 %collective-permute-start = (bf16[1,8,128]{2,1,0:T(8,128)(2,1)S(1)}, bf16[1,8,128]{2,1,0:T(8,128)(2,1)S(1)}, u32[]{:S(2)}, u32[]{:S(2)}) collective-permute-start(bf16[1,8,128]{2,1,0:T(8,128)(2,1)S(1)} %copy.26), channel_id=1, source_target_pairs={{240,0},{0,16},{16,32},{32,48},{48,64},{64,80},{80,96},{96,112},{1... | collective-permute-start | bytes 6152 | tf_op jit(solution)/shard_map/while/body/eval_jaxpr/ppermute | solution.py:12
  178.4 7.2 %collective-permute-start.1 = (f32[1,8]{1,0:T(1,128)S(1)}, f32[1,8]{1,0:T(1,128)S(1)}, u32[]{:S(2)}, u32[]{:S(2)}) collective-permute-start(f32[1,8]{1,0:T(1,128)S(1)} %get-tuple-element.331), channel_id=1, source_target_pairs={{240,0},{0,16},{16,32},{32,48},{48,64},{64,80},{80,96},{96,112},{1... | collective-permute-start | bytes 104 | tf_op jit(solution)/shard_map/while/body/eval_jaxpr/ppermute | solution.py:12
  195.5 10.3 %collective-permute-start.3 = (f32[1,8,128]{2,1,0:T(8,128)S(1)}, f32[1,8,128]{2,1,0:T(8,128)S(1)}, u32[]{:S(2)}, u32[]{:S(2)}) collective-permute-start(f32[1,8,128]{2,1,0:T(8,128)S(1)} %fusion.28), channel_id=1, source_target_pairs={{240,0},{0,16},{16,32},{32,48},{48,64},{64,80},{80,96},{96,112},{1... | collective-permute-start | bytes 12296 | tf_op jit(solution)/shard_map/while/body/eval_jaxpr/ppermute | solution.py:12
  197.5 8.3 %collective-permute-start = (bf16[1,8,128]{2,1,0:T(8,128)(2,1)S(1)}, bf16[1,8,128]{2,1,0:T(8,128)(2,1)S(1)}, u32[]{:S(2)}, u32[]{:S(2)}) collective-permute-start(bf16[1,8,128]{2,1,0:T(8,128)(2,1)S(1)} %copy.26), channel_id=1, source_target_pairs={{240,0},{0,16},{16,32},{32,48},{48,64},{64,80},{80,96},{96,112},{1... | collective-permute-start | bytes 6152 | tf_op jit(solution)/shard_map/while/body/eval_jaxpr/ppermute | solution.py:12
  213.7 7.2 %collective-permute-start.3 = (f32[1,8,128]{2,1,0:T(8,128)S(1)}, f32[1,8,128]{2,1,0:T(8,128)S(1)}, u32[]{:S(2)}, u32[]{:S(2)}) collective-permute-start(f32[1,8,128]{2,1,0:T(8,128)S(1)} %fusion.28), channel_id=1, source_target_pairs={{240,0},{0,16},{16,32},{32,48},{48,64},{64,80},{80,96},{96,112},{1... | collective-permute-start | bytes 12296 | tf_op jit(solution)/shard_map/while/body/eval_jaxpr/ppermute | solution.py:12
  228.8 11.4 %collective-permute-start.3 = (f32[1,8,128]{2,1,0:T(8,128)S(1)}, f32[1,8,128]{2,1,0:T(8,128)S(1)}, u32[]{:S(2)}, u32[]{:S(2)}) collective-permute-start(f32[1,8,128]{2,1,0:T(8,128)S(1)} %fusion.28), channel_id=1, source_target_pairs={{240,0},{0,16},{16,32},{32,48},{48,64},{64,80},{80,96},{96,112},{1... | collective-permute-start | bytes 12296 | tf_op jit(solution)/shard_map/while/body/eval_jaxpr/ppermute | solution.py:12
  228.9 11.4 %collective-permute-start = (bf16[1,8,128]{2,1,0:T(8,128)(2,1)S(1)}, bf16[1,8,128]{2,1,0:T(8,128)(2,1)S(1)}, u32[]{:S(2)}, u32[]{:S(2)}) collective-permute-start(bf16[1,8,128]{2,1,0:T(8,128)(2,1)S(1)} %copy.26), channel_id=1, source_target_pairs={{240,0},{0,16},{16,32},{32,48},{48,64},{64,80},{80,96},{96,112},{1... | collective-permute-start | bytes 6152 | tf_op jit(solution)/shard_map/while/body/eval_jaxpr/ppermute | solution.py:12
  248.2 8.4 %collective-permute-start.3 = (f32[1,8,128]{2,1,0:T(8,128)S(1)}, f32[1,8,128]{2,1,0:T(8,128)S(1)}, u32[]{:S(2)}, u32[]{:S(2)}) collective-permute-start(f32[1,8,128]{2,1,0:T(8,128)S(1)} %fusion.28), channel_id=1, source_target_pairs={{240,0},{0,16},{16,32},{32,48},{48,64},{64,80},{80,96},{96,112},{1... | collective-permute-start | bytes 12296 | tf_op jit(solution)/shard_map/while/body/eval_jaxpr/ppermute | solution.py:12
  248.3 8.3 %collective-permute-start = (bf16[1,8,128]{2,1,0:T(8,128)(2,1)S(1)}, bf16[1,8,128]{2,1,0:T(8,128)(2,1)S(1)}, u32[]{:S(2)}, u32[]{:S(2)}) collective-permute-start(bf16[1,8,128]{2,1,0:T(8,128)(2,1)S(1)} %copy.26), channel_id=1, source_target_pairs={{240,0},{0,16},{16,32},{32,48},{48,64},{64,80},{80,96},{96,112},{1... | collective-permute-start | bytes 6152 | tf_op jit(solution)/shard_map/while/body/eval_jaxpr/ppermute | solution.py:12
  264.5 10.7 %collective-permute-start.3 = (f32[1,8,128]{2,1,0:T(8,128)S(1)}, f32[1,8,128]{2,1,0:T(8,128)S(1)}, u32[]{:S(2)}, u32[]{:S(2)}) collective-permute-start(f32[1,8,128]{2,1,0:T(8,128)S(1)} %fusion.28), channel_id=1, source_target_pairs={{240,0},{0,16},{16,32},{32,48},{48,64},{64,80},{80,96},{96,112},{1... | collective-permute-start | bytes 12296 | tf_op jit(solution)/shard_map/while/body/eval_jaxpr/ppermute | solution.py:12
  264.6 10.6 %collective-permute-start = (bf16[1,8,128]{2,1,0:T(8,128)(2,1)S(1)}, bf16[1,8,128]{2,1,0:T(8,128)(2,1)S(1)}, u32[]{:S(2)}, u32[]{:S(2)}) collective-permute-start(bf16[1,8,128]{2,1,0:T(8,128)(2,1)S(1)} %copy.26), channel_id=1, source_target_pairs={{240,0},{0,16},{16,32},{32,48},{48,64},{64,80},{80,96},{96,112},{1... | collective-permute-start | bytes 6152 | tf_op jit(solution)/shard_map/while/body/eval_jaxpr/ppermute | solution.py:12
  266.0 7.2 %collective-permute-start.1 = (f32[1,8]{1,0:T(1,128)S(1)}, f32[1,8]{1,0:T(1,128)S(1)}, u32[]{:S(2)}, u32[]{:S(2)}) collective-permute-start(f32[1,8]{1,0:T(1,128)S(1)} %get-tuple-element.331), channel_id=1, source_target_pairs={{240,0},{0,16},{16,32},{32,48},{48,64},{64,80},{80,96},{96,112},{1... | collective-permute-start | bytes 104 | tf_op jit(solution)/shard_map/while/body/eval_jaxpr/ppermute | solution.py:12
  283.1 12.2 %collective-permute-start.3 = (f32[1,8,128]{2,1,0:T(8,128)S(1)}, f32[1,8,128]{2,1,0:T(8,128)S(1)}, u32[]{:S(2)}, u32[]{:S(2)}) collective-permute-start(f32[1,8,128]{2,1,0:T(8,128)S(1)} %fusion.28), channel_id=1, source_target_pairs={{240,0},{0,16},{16,32},{32,48},{48,64},{64,80},{80,96},{96,112},{1... | collective-permute-start | bytes 12296 | tf_op jit(solution)/shard_map/while/body/eval_jaxpr/ppermute | solution.py:12
  285.4 9.9 %collective-permute-start = (bf16[1,8,128]{2,1,0:T(8,128)(2,1)S(1)}, bf16[1,8,128]{2,1,0:T(8,128)(2,1)S(1)}, u32[]{:S(2)}, u32[]{:S(2)}) collective-permute-start(bf16[1,8,128]{2,1,0:T(8,128)(2,1)S(1)} %copy.26), channel_id=1, source_target_pairs={{240,0},{0,16},{16,32},{32,48},{48,64},{64,80},{80,96},{96,112},{1... | collective-permute-start | bytes 6152 | tf_op jit(solution)/shard_map/while/body/eval_jaxpr/ppermute | solution.py:12
  303.3 8.7 %collective-permute-start.3 = (f32[1,8,128]{2,1,0:T(8,128)S(1)}, f32[1,8,128]{2,1,0:T(8,128)S(1)}, u32[]{:S(2)}, u32[]{:S(2)}) collective-permute-start(f32[1,8,128]{2,1,0:T(8,128)S(1)} %fusion.28), channel_id=1, source_target_pairs={{240,0},{0,16},{16,32},{32,48},{48,64},{64,80},{80,96},{96,112},{1... | collective-permute-start | bytes 12296 | tf_op jit(solution)/shard_map/while/body/eval_jaxpr/ppermute | solution.py:12
  303.3 8.6 %collective-permute-start = (bf16[1,8,128]{2,1,0:T(8,128)(2,1)S(1)}, bf16[1,8,128]{2,1,0:T(8,128)(2,1)S(1)}, u32[]{:S(2)}, u32[]{:S(2)}) collective-permute-start(bf16[1,8,128]{2,1,0:T(8,128)(2,1)S(1)} %copy.26), channel_id=1, source_target_pairs={{240,0},{0,16},{16,32},{32,48},{48,64},{64,80},{80,96},{96,112},{1... | collective-permute-start | bytes 6152 | tf_op jit(solution)/shard_map/while/body/eval_jaxpr/ppermute | solution.py:12
  319.8 8.1 %collective-permute-start.3 = (f32[1,8,128]{2,1,0:T(8,128)S(1)}, f32[1,8,128]{2,1,0:T(8,128)S(1)}, u32[]{:S(2)}, u32[]{:S(2)}) collective-permute-start(f32[1,8,128]{2,1,0:T(8,128)S(1)} %fusion.28), channel_id=1, source_target_pairs={{240,0},{0,16},{16,32},{32,48},{48,64},{64,80},{80,96},{96,112},{1... | collective-permute-start | bytes 12296 | tf_op jit(solution)/shard_map/while/body/eval_jaxpr/ppermute | solution.py:12
  319.9 8.1 %collective-permute-start = (bf16[1,8,128]{2,1,0:T(8,128)(2,1)S(1)}, bf16[1,8,128]{2,1,0:T(8,128)(2,1)S(1)}, u32[]{:S(2)}, u32[]{:S(2)}) collective-permute-start(bf16[1,8,128]{2,1,0:T(8,128)(2,1)S(1)} %copy.26), channel_id=1, source_target_pairs={{240,0},{0,16},{16,32},{32,48},{48,64},{64,80},{80,96},{96,112},{1... | collective-permute-start | bytes 6152 | tf_op jit(solution)/shard_map/while/body/eval_jaxpr/ppermute | solution.py:12
  (37 other events, 601.1 us)
where the time goes:
time: 453 us; the launch traced here: 450 us
  blocking collectives  118 us (26%)
  starting transfers between devices  115 us (25%)
  local copies, waits for them, and re-layouts  85.7 us (19%)
  waiting for transfers between devices  77.8 us (17%)
  other arithmetic  40.4 us (9%)
  matrix products  11.7 us (3%)
    ppermute x65, starting transfers between devices, passed_along(): return lax.ppermute(block, axis, route)  115 us
    unnamed x1, blocking collectives  86.8 us
    ppermute x65, waiting for transfers between devices, passed_along(): return lax.ppermute(block, axis, route)  77.8 us
    gather x16, local copies, waits for them, and re-layouts, local_partial(): pages = jnp.take(page_pool, page_slots, axis=0)  66.9 us
    all_gather x1, blocking collectives, body(): piece = lax.all_gather(attended, 'inst', axis=0, tiled=True)  31.4 us
    select_n x32, other arithmetic, local_partial(): pages = jnp.take(page_pool, page_slots, axis=0)  12.4 us
    lt x16, other arithmetic, local_partial(): token_live = positions[None, :, :] < live_counts[:, None, None]  11.1 us
    and x16, other arithmetic, local_partial(): pages = jnp.take(page_pool, page_slots, axis=0)  10.6 us
  transfers between devices with their start and end apart: 65, of which 29 were waited for; matrix products, arithmetic and copies ran while one was open for 29% of the time, Pallas kernels for 0%

commit v1 on v0

v1 whole, which is shorter than its diff:
```python
import jax
import jax.numpy as jnp
from jax import lax
from jax.experimental import pallas as pl
from jax.experimental.pallas import tpu as pltpu
from jax.sharding import PartitionSpec as P

NEG_BIG = -1e30
STAT_ROWS = 16


def gather_pages(page_pool, move_slots, parity_axis, cuts):
    half = sum(cuts)
    firsts = [sum(cuts[:k]) for k in range(len(cuts))]

    def kernel(slots_ref, pool_ref, *rest):
        piece_refs, sems = rest[:-1], rest[-1]
        first = lax.rem(lax.axis_index(parity_axis), 2) * half
        moves = [
            pltpu.make_async_copy(
                pool_ref.at[slots_ref[0, first + at + k]], ref.at[k], sems.at[at + k]
            )
            for at, cut, ref in zip(firsts, cuts, piece_refs)
            for k in range(cut)
        ]
        for move in moves:
            move.start()
        for move in moves:
            move.wait()

    return pl.pallas_call(
        kernel,
        out_shape=[
            jax.ShapeDtypeStruct((cut,) + page_pool.shape[1:], page_pool.dtype) for cut in cuts
        ],
        in_specs=[
            pl.BlockSpec(memory_space=pltpu.SMEM),
            pl.BlockSpec(memory_space=pl.ANY),
        ],
        out_specs=[pl.BlockSpec(memory_space=pltpu.VMEM)] * len(cuts),
        scratch_shapes=[pltpu.SemaphoreType.DMA((half,))],
        compiler_params=pltpu.CompilerParams(vmem_limit_bytes=58 * 1024 * 1024),
        name="gather_pages",
    )(move_slots, page_pool)


def join_pieces(mine, theirs, parity_axis):
    cuts = [piece.shape[0] for piece in mine]
    half = sum(cuts)
    firsts = [sum(cuts[:k]) for k in range(len(cuts))]
    many = len(cuts)

    def kernel(*refs):
        mine_refs, theirs_refs = refs[:many], refs[many : 2 * many]
        out_ref, sems = refs[2 * many :]
        parity = lax.rem(lax.axis_index(parity_axis), 2)
        moves = []
        for side, pieces in ((parity, mine_refs), (1 - parity, theirs_refs)):
            for at, cut, ref in zip(firsts, cuts, pieces):
                rows = pl.ds(side * half + at, cut)
                moves.append(pltpu.make_async_copy(ref, out_ref.at[rows], sems.at[len(moves)]))
        for move in moves:
            move.start()
        for move in moves:
            move.wait()

    return pl.pallas_call(
        kernel,
        out_shape=jax.ShapeDtypeStruct((2 * half,) + mine[0].shape[1:], mine[0].dtype),
        in_specs=[pl.BlockSpec(memory_space=pltpu.VMEM)] * (2 * many),
        out_specs=pl.BlockSpec(memory_space=pl.ANY),
        scratch_shapes=[pltpu.SemaphoreType.DMA((2 * many,))],
        compiler_params=pltpu.CompilerParams(vmem_limit_bytes=4 * 1024 * 1024),
        name="join_pieces",
    )(*mine, *theirs)


def attend(queries, page_pool, block_tables, token_counts):
    requests, heads, size = queries.shape
    pages = block_tables.shape[1]
    page_len = page_pool.shape[3]
    tokens = pages * page_len
    rows = requests * heads
    scale = 1.0 / size**0.5

    def kernel(tables_ref, counts_ref, queries_ref, pool_ref, out_ref, query_ref, score_ref):
        for r in range(requests):
            query_ref[pl.ds(r, heads, stride=requests), :] = queries_ref[r].astype(jnp.float32)
        turned = jnp.transpose(query_ref[...]).astype(jnp.bfloat16)
        lane = lax.rem(lax.broadcasted_iota(jnp.int32, (1, rows), 1), requests)
        limit = jnp.zeros((1, rows), jnp.int32)
        for r in range(requests):
            limit = jnp.where(lane == r, counts_ref[r], limit)
        for r in range(requests):
            keys = jnp.concatenate([pool_ref[tables_ref[r, j], 0, 0] for j in range(pages)], axis=0)
            tile = jnp.dot(keys, turned, preferred_element_type=jnp.float32)
            score_ref[...] = tile if r == 0 else jnp.where(lane == r, tile, score_ref[...])
        position = lax.broadcasted_iota(jnp.int32, (tokens, rows), 0)
        scores = jnp.where(position < limit, score_ref[...] * scale, NEG_BIG)
        top = jnp.max(scores, axis=0, keepdims=True)
        weights = jnp.exp(scores - top).astype(jnp.bfloat16)
        total = jnp.sum(weights.astype(jnp.float32), axis=0, keepdims=True)
        weights = jnp.transpose(weights)
        row = lax.rem(lax.broadcasted_iota(jnp.int32, (rows, size), 0), requests)
        out = jnp.zeros((rows, size), jnp.float32)
        for r in range(requests):
            values = jnp.concatenate(
                [pool_ref[tables_ref[r, j], 1, 0] for j in range(pages)], axis=0
            )
            share = jnp.dot(weights, values, preferred_element_type=jnp.float32)
            out = jnp.where(row == r, share, out)
        out_ref[pl.ds(0, rows), :] = out / jnp.transpose(jnp.broadcast_to(total, (rows, rows)))
        out_ref[pl.ds(rows, 8), :] = jnp.broadcast_to(top + jnp.log(total), (8, rows))

    return pl.pallas_call(
        kernel,
        out_shape=jax.ShapeDtypeStruct((rows + 8, size), jnp.float32),
        in_specs=[
            pl.BlockSpec(memory_space=pltpu.SMEM),
            pl.BlockSpec(memory_space=pltpu.SMEM),
            pl.BlockSpec(memory_space=pltpu.VMEM),
            pl.BlockSpec(memory_space=pltpu.VMEM),
        ],
        out_specs=pl.BlockSpec(memory_space=pltpu.VMEM),
        scratch_shapes=[
            pltpu.VMEM((rows, size), jnp.float32),
            pltpu.VMEM((tokens, rows), jnp.float32),
        ],
        compiler_params=pltpu.CompilerParams(vmem_limit_bytes=16 * 1024 * 1024),
        name="attend",
    )(block_tables, token_counts, queries, page_pool)


def merge_two(mine, theirs, copies):
    rows, size = mine.shape[0] - 8, mine.shape[1]

    def kernel(mine_ref, theirs_ref, out_ref):
        log_one = mine_ref[pl.ds(rows, 1), :]
        log_two = theirs_ref[pl.ds(rows, 1), :]
        top = jnp.maximum(log_one, log_two)
        one = jnp.exp(log_one - top)
        two = jnp.exp(log_two - top)
        total = one + two
        logs = top + jnp.log(total)
        weight = jnp.transpose(jnp.broadcast_to(one / total, (rows, rows)))
        other = jnp.transpose(jnp.broadcast_to(two / total, (rows, rows)))
        parts = weight * mine_ref[pl.ds(0, rows), :] + other * theirs_ref[pl.ds(0, rows), :]
        high = logs.astype(jnp.bfloat16).astype(jnp.float32)
        middle = (logs - high).astype(jnp.bfloat16).astype(jnp.float32)
        low = logs - high - middle
        row = lax.broadcasted_iota(jnp.int32, (STAT_ROWS, rows), 0)
        stats = jnp.where(row == 0, high, jnp.where(row == 1, middle, jnp.where(row == 2, low, 0.0)))
        parts = parts.astype(jnp.bfloat16)
        stats = stats.astype(jnp.bfloat16)
        for i in range(copies):
            out_ref[i, pl.ds(0, rows), :] = parts
            out_ref[i, pl.ds(rows, STAT_ROWS), :] = stats

    return pl.pallas_call(
        kernel,
        out_shape=jax.ShapeDtypeStruct((copies, rows + STAT_ROWS, size), jnp.bfloat16),
        in_specs=[pl.BlockSpec(memory_space=pltpu.VMEM)] * 2,
        out_specs=pl.BlockSpec(memory_space=pltpu.VMEM),
        compiler_params=pltpu.CompilerParams(vmem_limit_bytes=4 * 1024 * 1024),
        name="merge_two",
    )(mine, theirs)


def combine_and_project(parts, out_weight, requests, heads):
    sources, _, size = parts.shape
    rows = requests * heads
    columns = out_weight.shape[1]
    folds = columns // size

    def kernel(parts_ref, weight_ref, out_ref):
        stats = parts_ref[:, pl.ds(rows, STAT_ROWS), :].astype(jnp.float32)
        logs = stats[:, 0, :] + stats[:, 1, :] + stats[:, 2, :]
        share = jnp.exp(logs - jnp.max(logs, axis=0, keepdims=True))
        share = share / jnp.sum(share, axis=0, keepdims=True)
        share = jnp.transpose(share)
        total = jnp.zeros((rows, size), jnp.float32)
        for i in range(sources):
            total += share[:, i : i + 1] * parts_ref[i, pl.ds(0, rows), :].astype(jnp.float32)
        attended = total.astype(jnp.bfloat16)
        attended = jnp.concatenate(
            [attended[h * requests : (h + 1) * requests] for h in range(heads)], axis=1
        )
        terms = jnp.dot(attended, weight_ref[...], preferred_element_type=jnp.float32)
        for c in range(folds):
            out_ref[pl.ds(c, requests, stride=folds), :] = terms[:, c * size : (c + 1) * size]

    return pl.pallas_call(
        kernel,
        out_shape=jax.ShapeDtypeStruct((requests * folds, size), jnp.float32),
        in_specs=[pl.BlockSpec(memory_space=pltpu.VMEM)] * 2,
        out_specs=pl.BlockSpec(memory_space=pltpu.VMEM),
        compiler_params=pltpu.CompilerParams(vmem_limit_bytes=16 * 1024 * 1024),
        name="combine_and_project",
    )(parts, out_weight)


def sum_terms(terms):
    _, folds, size = terms.shape

    def kernel(terms_ref, out_ref):
        total = jnp.sum(terms_ref[...], axis=0).astype(jnp.bfloat16)
        for c in range(folds):
            out_ref[:, pl.ds(c * size, size)] = total[c : c + 1, :]

    return pl.pallas_call(
        kernel,
        out_shape=jax.ShapeDtypeStruct((1, folds * size), jnp.bfloat16),
        in_specs=[pl.BlockSpec(memory_space=pltpu.VMEM)],
        out_specs=pl.BlockSpec(memory_space=pltpu.VMEM),
        compiler_params=pltpu.CompilerParams(vmem_limit_bytes=2 * 1024 * 1024),
        name="sum_terms",
    )(terms)


def body(queries, page_pool, block_tables, token_counts, move_slots, out_weight):
    instances = lax.axis_size("inst")
    devices = lax.axis_size("head")
    heads, size = queries.shape[1:]
    requests = instances * queries.shape[0]

    half = move_slots.shape[1] // 2
    cuts = (half - half // 2, half // 2)
    far = [(i, (i + instances // 2) % instances) for i in range(instances)]
    side = [(i, i ^ 1) for i in range(instances)]
    pair = [(i, i ^ 1) for i in range(devices)]
    rings = [[2 * k + s for k in range(instances // 2)] for s in range(2)]

    copies = jnp.broadcast_to(queries, (instances, heads, size))
    all_queries = lax.all_to_all(copies, "inst", 0, 0, tiled=True)
    first, second = gather_pages(page_pool, move_slots, "head", cuts)

    first, all_queries = lax.optimization_barrier((first, all_queries))
    first = lax.ppermute(first, "inst", far)
    parts = attend(all_queries, page_pool, block_tables[:, 0, :], token_counts[:, 0])
    others = lax.ppermute(parts, "inst", side)
    parts = merge_two(parts, others, instances // 2)
    first, parts = lax.optimization_barrier((first, parts))
    first_too = lax.ppermute(first, "head", pair)
    parts = lax.all_to_all(parts, "inst", 0, 0, tiled=True, axis_index_groups=rings)

    second, parts = lax.optimization_barrier((second, parts))
    second = lax.ppermute(second, "inst", far)
    terms = combine_and_project(parts, out_weight, requests, heads)
    terms = terms.reshape(devices, terms.shape[0] // devices, size)
    terms = lax.all_to_all(terms, "head", 0, 0, tiled=True)
    second, terms = lax.optimization_barrier((second, terms))
    second_too = lax.ppermute(second, "head", pair)
    arrived = join_pieces((first, second), (first_too, second_too), "head")
    return (sum_terms(terms), arrived)


def solution(mesh):
    in_specs = (
        P("inst", "head", None),
        P("inst", None, "head", None, None),
        P(None, "inst", None),
        P(None, "inst"),
        P("inst", None),
        P("head", "inst"),
    )
    out_specs = (P("head", "inst"), P("inst", None, "head", None, None))
    return jax.shard_map(body, mesh=mesh, in_specs=in_specs, out_specs=out_specs, check_vma=False)
```

time: 453 us -> 70.7 us (0.16)
  blocking collectives: 118 us -> 16.1 us
  starting transfers between devices: 115 us -> 23.1 us
  local copies, waits for them, and re-layouts: 85.7 us -> 4.85 us
  waiting for transfers between devices: 77.8 us -> 16.5 us
  other arithmetic: 40.4 us -> 0 us
  matrix products: 11.7 us -> 0 us
  Pallas kernels: 0 us -> 9.14 us
    ppermute x65 -> x5, starting transfers between devices: 115 us -> 2.67 us  [the longest x1 1.14 us: body(): others = lax.ppermute(parts, 'inst', side)]
    unnamed x1 -> x0, blocking collectives: 86.8 us -> none
    ppermute x65 -> x5, waiting for transfers between devices: 77.8 us -> 4.46 us  [the longest x1 3.91 us: body(): others = lax.ppermute(parts, 'inst', side)]
    gather x17 -> x0, local copies, waits for them, and re-layouts: 71.1 us -> none  [the longest x16 66.9 us: local_partial(): pages = jnp.take(page_pool, page_slots, axis=0)]
    all_gather x1 -> x0, blocking collectives: 31.4 us -> none  [body(): piece = lax.all_gather(attended, 'inst', axis=0, tiled=True)]
    all_to_all x0 -> x2, starting transfers between devices: none -> 20.4 us  [the longest x1 11.6 us: body(): all_queries = lax.all_to_all(copies, 'inst', 0, 0, tiled=True)]
    all_to_all x0 -> x1, blocking collectives: none -> 16.1 us  [body(): lax.all_to_all(parts, 'inst', 0, 0, tiled=True, axis_index_groups=rings)]
    select_n x34 -> x0, other arithmetic: 14.3 us -> none  [the longest x32 12.4 us: local_partial(): pages = jnp.take(page_pool, page_slots, axis=0)]
  transfers between devices with their start and end apart: 65 -> 7, of which waited for: 29 -> 4; matrix products, arithmetic and copies ran while one was open for 29% -> 0% of each run, Pallas kernels for 0% -> 12%
where the time goes in v1:
time: 70.7 us; the launch traced here: 70.4 us
  starting transfers between devices  23.1 us (33%)
  waiting for transfers between devices  16.5 us (23%)
  blocking collectives  16.1 us (23%)
  Pallas kernels  9.14 us (13%)
  local copies, waits for them, and re-layouts  4.85 us (7%)
    all_to_all x1, blocking collectives, body(): lax.all_to_all(parts, 'inst', 0, 0, tiled=True, axis_index_groups=rings)  16.1 us
    all_to_all x1, starting transfers between devices, body(): all_queries = lax.all_to_all(copies, 'inst', 0, 0, tiled=True)  11.6 us
    all_to_all x1, starting transfers between devices, body(): terms = lax.all_to_all(terms, 'head', 0, 0, tiled=True)  8.84 us
    all_to_all x1, waiting for transfers between devices, body(): all_queries = lax.all_to_all(copies, 'inst', 0, 0, tiled=True)  6.37 us
    all_to_all x1, waiting for transfers between devices, body(): terms = lax.all_to_all(terms, 'head', 0, 0, tiled=True)  5.64 us
    ppermute x1, waiting for transfers between devices, body(): others = lax.ppermute(parts, 'inst', side)  3.91 us
    unnamed x10, local copies, waits for them, and re-layouts  3.55 us
    pallas_call x1, Pallas kernels, attend(): pl.pallas_call(kernel, out_shape=jax.ShapeDtypeStruct((rows + 8, size), j...  3.4 us
  transfers between devices with their start and end apart: 7, of which 4 were waited for; matrix products, arithmetic and copies ran while one was open for 0% of the time, Pallas kernels for 12%

profile of v1, /device:TPU:1, one launch (start us, length us, event | category | flops | bytes accessed | tf_op | source)
XLA Modules:
  0.0 70.4 jit_solution(10484841521888885350)
XLA Ops:
  0.6 0.0 copy-start.3
  0.6 0.0 copy-start.2
  0.6 1.3 %broadcast_in_dim.8 = bf16[16,8,128]{2,1,0:T(8,128)(2,1)} broadcast(bf16[8,128]{1,0:T(8,128)(2,1)} %bitcast.6), dimensions={1,2} | broadcast | bytes 34816 | tf_op jit(solution)/shard_map/broadcast_in_dim | solution.py:233
  2.0 11.6 %all-to-all-start = ((bf16[16,8,128]{2,1,0:T(8,128)(2,1)}), bf16[16,8,128]{2,1,0:T(8,128)(2,1)S(1)}, u32[]{:S(2)}, u32[]{:S(2)}) async-start(bf16[16,8,128]{2,1,0:T(8,128)(2,1)} %broadcast_in_dim.8), calls=%async_computation | async-start | bytes 65536 | tf_op jit(solution)/shard_map/all_to_all | solution.py:234
  13.5 0.0 copy-start.1
  13.6 2.7 %gather_pages.1 = (bf16[8,2,1,64,128]{4,3,2,1,0:T(8,128)(2,1)}, bf16[8,2,1,64,128]{4,3,2,1,0:T(8,128)(2,1)}) custom-call(s32[1,32]{1,0:T(1,128)} %slots_ref.1, bf16[272,2,1,64,128]{4,3,2,1,0:T(8,128)(2,1)} %pool_ref.3), custom_call_target="tpu_custom_call" | custom-call | tf_op jit(solution)/shard_map/gather_pages/pallas_call | solution.py:31
  16.3 6.4 %all-to-all-done.queries_ref = bf16[16,8,128]{2,1,0:T(8,128)(2,1)S(1)} async-done(((bf16[16,8,128]{2,1,0:T(8,128)(2,1)}), bf16[16,8,128]{2,1,0:T(8,128)(2,1)S(1)}, u32[]{:S(2)}, u32[]{:S(2)}) %all-to-all-start) | async-done | bytes 32800 | tf_op jit(solution)/shard_map/all_to_all | solution.py:234
  22.7 0.6 collective-permute-start
  23.3 0.0 copy-done.3
  23.3 0.0 copy-done.2
  23.3 0.0 copy-start
  23.3 3.5 %copy-done = bf16[272,2,1,64,128]{4,3,2,1,0:T(8,128)(2,1)S(1)} copy-done((bf16[272,2,1,64,128]{4,3,2,1,0:T(8,128)(2,1)S(1)}, bf16[272,2,1,64,128]{4,3,2,1,0:T(8,128)(2,1)}, u32[]{:S(2)}) %copy-start) | copy-done | bytes 8912920
  26.8 0.0 copy-start.4
  26.8 3.4 %attend.1.mine_ref = f32[136,128]{1,0:T(8,128)S(1)} custom-call(s32[16,16]{1,0:T(8,128)S(1)} %bitcast.4, s32[16]{0:T(128)S(1)} %bitcast.5, bf16[16,8,128]{2,1,0:T(8,128)(2,1)S(1)} %all-to-all-done.queries_ref, bf16[272,2,1,64,128]{4,3,2,1,0:T(8,128)(2,1)S(1)} %copy-done), custom_call_target="tpu_custom_call" | custom-call | tf_op jit(solution)/shard_map/attend/pallas_call | solution.py:115
  30.2 1.1 %collective-permute-start.1 = (f32[136,128]{1,0:T(8,128)S(1)}, f32[136,128]{1,0:T(8,128)S(1)}, u32[]{:S(2)}, u32[]{:S(2)}) collective-permute-start(f32[136,128]{1,0:T(8,128)S(1)} %attend.1.mine_ref), channel_id=1, source_target_pairs={{0,16},{16,0},{32,48},{48,32},{64,80},{80,64},{96,112},{112,96},{1... | collective-permute-start | bytes 208904 | tf_op jit(solution)/shard_map/ppermute | solution.py:240
  31.4 3.9 %collective-permute-done.1.theirs_ref = f32[136,128]{1,0:T(8,128)S(1)} collective-permute-done((f32[136,128]{1,0:T(8,128)S(1)}, f32[136,128]{1,0:T(8,128)S(1)}, u32[]{:S(2)}, u32[]{:S(2)}) %collective-permute-start.1) | collective-permute-done | bytes 69664 | tf_op jit(solution)/shard_map/ppermute | solution.py:240
  35.3 0.1 merge_two.1
  35.4 0.0 collective-permute-done.refs_0_
  35.4 16.1 %all_to_all.15.parts_ref = bf16[8,144,128]{2,1,0:T(8,128)(2,1)S(1)} all-to-all(bf16[8,144,128]{2,1,0:T(8,128)(2,1)S(1)} %merge_two.1), channel_id=1, replica_groups={{0,32,64,96,128,160,192,224},{16,48,80,112,144,176,208,240},{1,33,65,97..., dimensions={0} | all-to-all | bytes 589824 | tf_op jit(solution)/shard_map/all_to_all | solution.py:244
  51.6 0.0 copy-done.4
  51.6 0.3 collective-permute-start.2
  51.8 0.0 copy-done.1
  51.8 1.3 %combine_and_project.1 = f32[128,128]{1,0:T(8,128)} custom-call(bf16[8,144,128]{2,1,0:T(8,128)(2,1)S(1)} %all_to_all.15.parts_ref, bf16[1024,1024]{1,0:T(8,128)(2,1)S(1)} %copy-done.1), custom_call_target="tpu_custom_call" | custom-call | tf_op jit(solution)/shard_map/combine_and_project/pallas_call | solution.py:192
  53.1 8.8 %all-to-all-start.2 = ((f32[16,8,128]{2,1,0:T(8,128)}), f32[16,8,128]{2,1,0:T(8,128)S(1)}, u32[]{:S(2)}, u32[]{:S(2)}) async-start(f32[16,8,128]{2,1,0:T(8,128)} %bitcast.3), calls=%async_computation.2 | async-start | bytes 131072 | tf_op jit(solution)/shard_map/all_to_all | solution.py:250
  61.9 0.2 collective-permute-start.3
  62.1 5.6 %all-to-all-done.2.terms_ref = f32[16,8,128]{2,1,0:T(8,128)S(1)} async-done(((f32[16,8,128]{2,1,0:T(8,128)}), f32[16,8,128]{2,1,0:T(8,128)S(1)}, u32[]{:S(2)}, u32[]{:S(2)}) %all-to-all-start.2) | async-done | bytes 65568 | tf_op jit(solution)/shard_map/all_to_all | solution.py:250
  67.8 0.0 collective-permute-done.2.refs_1_
  67.8 0.4 collective-permute-start.4
  68.2 0.6 sum_terms.1
  68.8 0.0 collective-permute-done.3.refs_2_
  68.8 0.5 collective-permute-done.4.refs_3_
  69.4 1.0 %join_pieces.1 = bf16[32,2,1,64,128]{4,3,2,1,0:T(8,128)(2,1)} custom-call(bf16[8,2,1,64,128]{4,3,2,1,0:T(8,128)(2,1)S(1)} %collective-permute-done.refs_0_, bf16[8,2,1,64,128]{4,3,2,1,0:T(8,128)(2,1)S(1)} %collective-permute-done.2.refs_1_, bf16[8,2,1,64,128]{4,3,2,1,0:T(8,128)(2,1)S(1)} %collective-permute-done.3.refs_2_, ...), custom_call_target="tpu_custom_call" | custom-call | tf_op jit(solution)/shard_map/join_pieces/pallas_call | solution.py:67
Async XLA Ops:
  0.6 22.7 %copy-start.3 = (s32[16,1]{0,1:T(1,128)S(1)}, s32[16,1]{0,1:T(1,128)}, u32[]{:S(2)}) copy-start(s32[16,1]{0,1:T(1,128)} %param.9) | copy-start | bytes 196
  0.6 22.7 %copy-start.2 = (s32[16,1,16]{2,1,0:T(1,128)S(1)}, s32[16,1,16]{2,1,0:T(1,128)}, u32[]{:S(2)}) copy-start(s32[16,1,16]{2,1,0:T(1,128)} %param.8) | copy-start | bytes 3076
  2.0 20.7 %all-to-all-start = ((bf16[16,8,128]{2,1,0:T(8,128)(2,1)}), bf16[16,8,128]{2,1,0:T(8,128)(2,1)S(1)}, u32[]{:S(2)}, u32[]{:S(2)}) async-start(bf16[16,8,128]{2,1,0:T(8,128)(2,1)} %broadcast_in_dim.8), calls=%async_computation | async-start | bytes 65536 | tf_op jit(solution)/shard_map/all_to_all | solution.py:234
  13.5 38.3 %copy-start.1 = (bf16[1024,1024]{1,0:T(8,128)(2,1)S(1)}, bf16[1024,1024]{1,0:T(8,128)(2,1)}, u32[]{:S(2)}) copy-start(bf16[1024,1024]{1,0:T(8,128)(2,1)} %weight_ref.1) | copy-start | bytes 6291460
  22.7 12.8 %collective-permute-start = (bf16[8,2,1,64,128]{4,3,2,1,0:T(8,128)(2,1)}, bf16[8,2,1,64,128]{4,3,2,1,0:T(8,128)(2,1)S(1)}, u32[]{:S(2)}, u32[]{:S(2)}) collective-permute-start(bf16[8,2,1,64,128]{4,3,2,1,0:T(8,128)(2,1)} %get-tuple-element.14), channel_id=1, source_target_pairs={{0,128},{16,144},{32,160},{48,176},{64,192},{80,208},{96,224},{112... | collective-permute-start | bytes 786440 | tf_op jit(solution)/shard_map/ppermute | solution.py:238
  23.3 3.5 %copy-start = (bf16[272,2,1,64,128]{4,3,2,1,0:T(8,128)(2,1)S(1)}, bf16[272,2,1,64,128]{4,3,2,1,0:T(8,128)(2,1)}, u32[]{:S(2)}) copy-start(bf16[272,2,1,64,128]{4,3,2,1,0:T(8,128)(2,1)} %pool_ref.3) | copy-start | bytes 26738692
  26.8 24.7 %copy-start.4 = (bf16[8,2,1,64,128]{4,3,2,1,0:T(8,128)(2,1)S(1)}, bf16[8,2,1,64,128]{4,3,2,1,0:T(8,128)(2,1)}, u32[]{:S(2)}) copy-start(bf16[8,2,1,64,128]{4,3,2,1,0:T(8,128)(2,1)} %get-tuple-element.17) | copy-start | bytes 786436
  30.2 5.0 %collective-permute-start.1 = (f32[136,128]{1,0:T(8,128)S(1)}, f32[136,128]{1,0:T(8,128)S(1)}, u32[]{:S(2)}, u32[]{:S(2)}) collective-permute-start(f32[136,128]{1,0:T(8,128)S(1)} %attend.1.mine_ref), channel_id=1, source_target_pairs={{0,16},{16,0},{32,48},{48,32},{64,80},{80,64},{96,112},{112,96},{1... | collective-permute-start | bytes 208904 | tf_op jit(solution)/shard_map/ppermute | solution.py:240
  51.6 16.2 %collective-permute-start.2 = (bf16[8,2,1,64,128]{4,3,2,1,0:T(8,128)(2,1)S(1)}, bf16[8,2,1,64,128]{4,3,2,1,0:T(8,128)(2,1)S(1)}, u32[]{:S(2)}, u32[]{:S(2)}) collective-permute-start(bf16[8,2,1,64,128]{4,3,2,1,0:T(8,128)(2,1)S(1)} %copy-done.4), channel_id=1, source_target_pairs={{0,128},{16,144},{32,160},{48,176},{64,192},{80,208},{96,224},{112... | collective-permute-start | bytes 786440 | tf_op jit(solution)/shard_map/ppermute | solution.py:247
  53.1 14.7 %all-to-all-start.2 = ((f32[16,8,128]{2,1,0:T(8,128)}), f32[16,8,128]{2,1,0:T(8,128)S(1)}, u32[]{:S(2)}, u32[]{:S(2)}) async-start(f32[16,8,128]{2,1,0:T(8,128)} %bitcast.3), calls=%async_computation.2 | async-start | bytes 131072 | tf_op jit(solution)/shard_map/all_to_all | solution.py:250
  61.9 6.9 %collective-permute-start.3 = (bf16[8,2,1,64,128]{4,3,2,1,0:T(8,128)(2,1)S(1)}, bf16[8,2,1,64,128]{4,3,2,1,0:T(8,128)(2,1)S(1)}, u32[]{:S(2)}, u32[]{:S(2)}) collective-permute-start(bf16[8,2,1,64,128]{4,3,2,1,0:T(8,128)(2,1)S(1)} %collective-permute-done.refs_0_), channel_id=1, source_target_pairs={{0,1},{1,0},{2,3},{3,2},{4,5},{5,4},{6,7},{7,6},{8,9},{9,8},{10,11... | collective-permute-start | bytes 786440 | tf_op jit(solution)/shard_map/ppermute | solution.py:243
  67.8 1.6 %collective-permute-start.4 = (bf16[8,2,1,64,128]{4,3,2,1,0:T(8,128)(2,1)S(1)}, bf16[8,2,1,64,128]{4,3,2,1,0:T(8,128)(2,1)S(1)}, u32[]{:S(2)}, u32[]{:S(2)}) collective-permute-start(bf16[8,2,1,64,128]{4,3,2,1,0:T(8,128)(2,1)S(1)} %collective-permute-done.2.refs_1_), channel_id=1, source_target_pairs={{0,1},{1,0},{2,3},{3,2},{4,5},{5,4},{6,7},{7,6},{8,9},{9,8},{10,11... | collective-permute-start | bytes 786440 | tf_op jit(solution)/shard_map/ppermute | solution.py:252

commit v2 on v1

--- a/solution.py
+++ b/solution.py
@@ -243,10 +243,10 @@
     first_too = lax.ppermute(first, "head", pair)
     parts = lax.all_to_all(parts, "inst", 0, 0, tiled=True, axis_index_groups=rings)
 
-    second, parts = lax.optimization_barrier((second, parts))
-    second = lax.ppermute(second, "inst", far)
     terms = combine_and_project(parts, out_weight, requests, heads)
     terms = terms.reshape(devices, terms.shape[0] // devices, size)
+    second, terms = lax.optimization_barrier((second, terms))
+    second = lax.ppermute(second, "inst", far)
     terms = lax.all_to_all(terms, "head", 0, 0, tiled=True)
     second, terms = lax.optimization_barrier((second, terms))
     second_too = lax.ppermute(second, "head", pair)

time: 70.7 us -> 71.4 us (level)
  transfers between devices with their start and end apart: 7 -> 7, of which waited for: 4 -> 4; matrix products, arithmetic and copies ran while one was open for 0% -> 0% of each run, Pallas kernels for 12% -> 10%
where the time goes in v2:
time: 71.4 us; the launch traced here: 70.4 us
  starting transfers between devices  23.1 us (32%)
  waiting for transfers between devices  16.5 us (23%)
  blocking collectives  16.1 us (23%)
  Pallas kernels  9.14 us (13%)
  local copies, waits for them, and re-layouts  4.85 us (7%)
    all_to_all x1, blocking collectives, body(): lax.all_to_all(parts, 'inst', 0, 0, tiled=True, axis_index_groups=rings)  16.1 us
    all_to_all x1, starting transfers between devices, body(): all_queries = lax.all_to_all(copies, 'inst', 0, 0, tiled=True)  11.6 us
    all_to_all x1, starting transfers between devices, body(): terms = lax.all_to_all(terms, 'head', 0, 0, tiled=True)  8.84 us
    all_to_all x1, waiting for transfers between devices, body(): all_queries = lax.all_to_all(copies, 'inst', 0, 0, tiled=True)  6.37 us
    all_to_all x1, waiting for transfers between devices, body(): terms = lax.all_to_all(terms, 'head', 0, 0, tiled=True)  5.64 us
    ppermute x1, waiting for transfers between devices, body(): others = lax.ppermute(parts, 'inst', side)  3.91 us
    unnamed x10, local copies, waits for them, and re-layouts  3.55 us
    pallas_call x1, Pallas kernels, attend(): pl.pallas_call(kernel, out_shape=jax.ShapeDtypeStruct((rows + 8, size), j...  3.4 us
  transfers between devices with their start and end apart: 7, of which 4 were waited for; matrix products, arithmetic and copies ran while one was open for 0% of the time, Pallas kernels for 10%

profile of v2, /device:TPU:1, one launch (start us, length us, event | category | flops | bytes accessed | tf_op | source)
XLA Modules:
  0.0 70.4 jit_solution(242158909734989849)
XLA Ops:
  0.6 0.0 copy-start.3
  0.6 0.0 copy-start.2
  0.6 1.3 %broadcast_in_dim.8 = bf16[16,8,128]{2,1,0:T(8,128)(2,1)} broadcast(bf16[8,128]{1,0:T(8,128)(2,1)} %bitcast.6), dimensions={1,2} | broadcast | bytes 34816 | tf_op jit(solution)/shard_map/broadcast_in_dim | solution.py:233
  2.0 11.6 %all-to-all-start = ((bf16[16,8,128]{2,1,0:T(8,128)(2,1)}), bf16[16,8,128]{2,1,0:T(8,128)(2,1)S(1)}, u32[]{:S(2)}, u32[]{:S(2)}) async-start(bf16[16,8,128]{2,1,0:T(8,128)(2,1)} %broadcast_in_dim.8), calls=%async_computation | async-start | bytes 65536 | tf_op jit(solution)/shard_map/all_to_all | solution.py:234
  13.5 0.0 copy-start.1
  13.6 2.7 %gather_pages.1 = (bf16[8,2,1,64,128]{4,3,2,1,0:T(8,128)(2,1)}, bf16[8,2,1,64,128]{4,3,2,1,0:T(8,128)(2,1)}) custom-call(s32[1,32]{1,0:T(1,128)} %slots_ref.1, bf16[272,2,1,64,128]{4,3,2,1,0:T(8,128)(2,1)} %pool_ref.3), custom_call_target="tpu_custom_call" | custom-call | tf_op jit(solution)/shard_map/gather_pages/pallas_call | solution.py:31
  16.3 6.4 %all-to-all-done.queries_ref = bf16[16,8,128]{2,1,0:T(8,128)(2,1)S(1)} async-done(((bf16[16,8,128]{2,1,0:T(8,128)(2,1)}), bf16[16,8,128]{2,1,0:T(8,128)(2,1)S(1)}, u32[]{:S(2)}, u32[]{:S(2)}) %all-to-all-start) | async-done | bytes 32800 | tf_op jit(solution)/shard_map/all_to_all | solution.py:234
  22.7 0.6 collective-permute-start
  23.3 0.0 copy-done.3
  23.3 0.0 copy-done.2
  23.3 0.0 copy-start
  23.3 3.5 %copy-done = bf16[272,2,1,64,128]{4,3,2,1,0:T(8,128)(2,1)S(1)} copy-done((bf16[272,2,1,64,128]{4,3,2,1,0:T(8,128)(2,1)S(1)}, bf16[272,2,1,64,128]{4,3,2,1,0:T(8,128)(2,1)}, u32[]{:S(2)}) %copy-start) | copy-done | bytes 8912920
  26.8 0.0 copy-start.4
  26.8 3.4 %attend.1.mine_ref = f32[136,128]{1,0:T(8,128)S(1)} custom-call(s32[16,16]{1,0:T(8,128)S(1)} %bitcast.4, s32[16]{0:T(128)S(1)} %bitcast.5, bf16[16,8,128]{2,1,0:T(8,128)(2,1)S(1)} %all-to-all-done.queries_ref, bf16[272,2,1,64,128]{4,3,2,1,0:T(8,128)(2,1)S(1)} %copy-done), custom_call_target="tpu_custom_call" | custom-call | tf_op jit(solution)/shard_map/attend/pallas_call | solution.py:115
  30.2 1.1 %collective-permute-start.1 = (f32[136,128]{1,0:T(8,128)S(1)}, f32[136,128]{1,0:T(8,128)S(1)}, u32[]{:S(2)}, u32[]{:S(2)}) collective-permute-start(f32[136,128]{1,0:T(8,128)S(1)} %attend.1.mine_ref), channel_id=1, source_target_pairs={{0,16},{16,0},{32,48},{48,32},{64,80},{80,64},{96,112},{112,96},{1... | collective-permute-start | bytes 208904 | tf_op jit(solution)/shard_map/ppermute | solution.py:240
  31.4 3.9 %collective-permute-done.1.theirs_ref = f32[136,128]{1,0:T(8,128)S(1)} collective-permute-done((f32[136,128]{1,0:T(8,128)S(1)}, f32[136,128]{1,0:T(8,128)S(1)}, u32[]{:S(2)}, u32[]{:S(2)}) %collective-permute-start.1) | collective-permute-done | bytes 69664 | tf_op jit(solution)/shard_map/ppermute | solution.py:240
  35.3 0.1 merge_two.1
  35.4 0.0 collective-permute-done.refs_0_
  35.4 16.1 %all_to_all.15.parts_ref = bf16[8,144,128]{2,1,0:T(8,128)(2,1)S(1)} all-to-all(bf16[8,144,128]{2,1,0:T(8,128)(2,1)S(1)} %merge_two.1), channel_id=1, replica_groups={{0,32,64,96,128,160,192,224},{16,48,80,112,144,176,208,240},{1,33,65,97..., dimensions={0} | all-to-all | bytes 589824 | tf_op jit(solution)/shard_map/all_to_all | solution.py:244
  51.6 0.0 copy-done.1
  51.6 1.3 %combine_and_project.1 = f32[128,128]{1,0:T(8,128)} custom-call(bf16[8,144,128]{2,1,0:T(8,128)(2,1)S(1)} %all_to_all.15.parts_ref, bf16[1024,1024]{1,0:T(8,128)(2,1)S(1)} %copy-done.1), custom_call_target="tpu_custom_call" | custom-call | tf_op jit(solution)/shard_map/combine_and_project/pallas_call | solution.py:192
  52.8 0.0 copy-done.4
  52.8 0.3 collective-permute-start.2
  53.1 8.8 %all-to-all-start.2 = ((f32[16,8,128]{2,1,0:T(8,128)}), f32[16,8,128]{2,1,0:T(8,128)S(1)}, u32[]{:S(2)}, u32[]{:S(2)}) async-start(f32[16,8,128]{2,1,0:T(8,128)} %bitcast.3), calls=%async_computation.2 | async-start | bytes 131072 | tf_op jit(solution)/shard_map/all_to_all | solution.py:250
  61.9 0.2 collective-permute-start.3
  62.1 5.6 %all-to-all-done.2.terms_ref = f32[16,8,128]{2,1,0:T(8,128)S(1)} async-done(((f32[16,8,128]{2,1,0:T(8,128)}), f32[16,8,128]{2,1,0:T(8,128)S(1)}, u32[]{:S(2)}, u32[]{:S(2)}) %all-to-all-start.2) | async-done | bytes 65568 | tf_op jit(solution)/shard_map/all_to_all | solution.py:250
  67.8 0.0 collective-permute-done.2.refs_1_
  67.8 0.4 collective-permute-start.4
  68.2 0.6 sum_terms.1
  68.8 0.0 collective-permute-done.3.refs_2_
  68.8 0.5 collective-permute-done.4.refs_3_
  69.4 1.0 %join_pieces.1 = bf16[32,2,1,64,128]{4,3,2,1,0:T(8,128)(2,1)} custom-call(bf16[8,2,1,64,128]{4,3,2,1,0:T(8,128)(2,1)S(1)} %collective-permute-done.refs_0_, bf16[8,2,1,64,128]{4,3,2,1,0:T(8,128)(2,1)S(1)} %collective-permute-done.2.refs_1_, bf16[8,2,1,64,128]{4,3,2,1,0:T(8,128)(2,1)S(1)} %collective-permute-done.3.refs_2_, ...), custom_call_target="tpu_custom_call" | custom-call | tf_op jit(solution)/shard_map/join_pieces/pallas_call | solution.py:67
Async XLA Ops:
  0.6 22.7 %copy-start.3 = (s32[16,1]{0,1:T(1,128)S(1)}, s32[16,1]{0,1:T(1,128)}, u32[]{:S(2)}) copy-start(s32[16,1]{0,1:T(1,128)} %param.9) | copy-start | bytes 196
  0.6 22.7 %copy-start.2 = (s32[16,1,16]{2,1,0:T(1,128)S(1)}, s32[16,1,16]{2,1,0:T(1,128)}, u32[]{:S(2)}) copy-start(s32[16,1,16]{2,1,0:T(1,128)} %param.8) | copy-start | bytes 3076
  2.0 20.7 %all-to-all-start = ((bf16[16,8,128]{2,1,0:T(8,128)(2,1)}), bf16[16,8,128]{2,1,0:T(8,128)(2,1)S(1)}, u32[]{:S(2)}, u32[]{:S(2)}) async-start(bf16[16,8,128]{2,1,0:T(8,128)(2,1)} %broadcast_in_dim.8), calls=%async_computation | async-start | bytes 65536 | tf_op jit(solution)/shard_map/all_to_all | solution.py:234
  13.5 38.0 %copy-start.1 = (bf16[1024,1024]{1,0:T(8,128)(2,1)S(1)}, bf16[1024,1024]{1,0:T(8,128)(2,1)}, u32[]{:S(2)}) copy-start(bf16[1024,1024]{1,0:T(8,128)(2,1)} %weight_ref.1) | copy-start | bytes 6291460
  22.7 12.8 %collective-permute-start = (bf16[8,2,1,64,128]{4,3,2,1,0:T(8,128)(2,1)}, bf16[8,2,1,64,128]{4,3,2,1,0:T(8,128)(2,1)S(1)}, u32[]{:S(2)}, u32[]{:S(2)}) collective-permute-start(bf16[8,2,1,64,128]{4,3,2,1,0:T(8,128)(2,1)} %get-tuple-element.14), channel_id=1, source_target_pairs={{0,128},{16,144},{32,160},{48,176},{64,192},{80,208},{96,224},{112... | collective-permute-start | bytes 786440 | tf_op jit(solution)/shard_map/ppermute | solution.py:238
  23.3 3.5 %copy-start = (bf16[272,2,1,64,128]{4,3,2,1,0:T(8,128)(2,1)S(1)}, bf16[272,2,1,64,128]{4,3,2,1,0:T(8,128)(2,1)}, u32[]{:S(2)}) copy-start(bf16[272,2,1,64,128]{4,3,2,1,0:T(8,128)(2,1)} %pool_ref.3) | copy-start | bytes 26738692
  26.8 26.0 %copy-start.4 = (bf16[8,2,1,64,128]{4,3,2,1,0:T(8,128)(2,1)S(1)}, bf16[8,2,1,64,128]{4,3,2,1,0:T(8,128)(2,1)}, u32[]{:S(2)}) copy-start(bf16[8,2,1,64,128]{4,3,2,1,0:T(8,128)(2,1)} %get-tuple-element.17) | copy-start | bytes 786436
  30.2 5.0 %collective-permute-start.1 = (f32[136,128]{1,0:T(8,128)S(1)}, f32[136,128]{1,0:T(8,128)S(1)}, u32[]{:S(2)}, u32[]{:S(2)}) collective-permute-start(f32[136,128]{1,0:T(8,128)S(1)} %attend.1.mine_ref), channel_id=1, source_target_pairs={{0,16},{16,0},{32,48},{48,32},{64,80},{80,64},{96,112},{112,96},{1... | collective-permute-start | bytes 208904 | tf_op jit(solution)/shard_map/ppermute | solution.py:240
  52.8 14.9 %collective-permute-start.2 = (bf16[8,2,1,64,128]{4,3,2,1,0:T(8,128)(2,1)S(1)}, bf16[8,2,1,64,128]{4,3,2,1,0:T(8,128)(2,1)S(1)}, u32[]{:S(2)}, u32[]{:S(2)}) collective-permute-start(bf16[8,2,1,64,128]{4,3,2,1,0:T(8,128)(2,1)S(1)} %copy-done.4), channel_id=1, source_target_pairs={{0,128},{16,144},{32,160},{48,176},{64,192},{80,208},{96,224},{112... | collective-permute-start | bytes 786440 | tf_op jit(solution)/shard_map/ppermute | solution.py:249
  53.1 14.7 %all-to-all-start.2 = ((f32[16,8,128]{2,1,0:T(8,128)}), f32[16,8,128]{2,1,0:T(8,128)S(1)}, u32[]{:S(2)}, u32[]{:S(2)}) async-start(f32[16,8,128]{2,1,0:T(8,128)} %bitcast.3), calls=%async_computation.2 | async-start | bytes 131072 | tf_op jit(solution)/shard_map/all_to_all | solution.py:250
  61.9 6.9 %collective-permute-start.3 = (bf16[8,2,1,64,128]{4,3,2,1,0:T(8,128)(2,1)S(1)}, bf16[8,2,1,64,128]{4,3,2,1,0:T(8,128)(2,1)S(1)}, u32[]{:S(2)}, u32[]{:S(2)}) collective-permute-start(bf16[8,2,1,64,128]{4,3,2,1,0:T(8,128)(2,1)S(1)} %collective-permute-done.refs_0_), channel_id=1, source_target_pairs={{0,1},{1,0},{2,3},{3,2},{4,5},{5,4},{6,7},{7,6},{8,9},{9,8},{10,11... | collective-permute-start | bytes 786440 | tf_op jit(solution)/shard_map/ppermute | solution.py:243
  67.8 1.6 %collective-permute-start.4 = (bf16[8,2,1,64,128]{4,3,2,1,0:T(8,128)(2,1)S(1)}, bf16[8,2,1,64,128]{4,3,2,1,0:T(8,128)(2,1)S(1)}, u32[]{:S(2)}, u32[]{:S(2)}) collective-permute-start(bf16[8,2,1,64,128]{4,3,2,1,0:T(8,128)(2,1)S(1)} %collective-permute-done.2.refs_1_), channel_id=1, source_target_pairs={{0,1},{1,0},{2,3},{3,2},{4,5},{5,4},{6,7},{7,6},{8,9},{9,8},{10,11... | collective-permute-start | bytes 786440 | tf_op jit(solution)/shard_map/ppermute | solution.py:252

commit v3 on v1

--- a/solution.py
+++ b/solution.py
@@ -224,7 +224,7 @@
     requests = instances * queries.shape[0]
 
     half = move_slots.shape[1] // 2
-    cuts = (half - half // 2, half // 2)
+    cuts = (half - half * 7 // 16, half * 7 // 16)
     far = [(i, (i + instances // 2) % instances) for i in range(instances)]
     side = [(i, i ^ 1) for i in range(instances)]
     pair = [(i, i ^ 1) for i in range(devices)]

time: 70.7 us -> 71.1 us (level)
  blocking collectives: 16.1 us -> 28.3 us
  starting transfers between devices: 23.1 us -> 17.5 us
  waiting for transfers between devices: 16.5 us -> 11 us
    all_to_all x0 -> x1, blocking collectives: none -> 10.2 us  [body(): terms = lax.all_to_all(terms, 'head', 0, 0, tiled=True)]
    all_to_all x1 -> x0, starting transfers between devices: 8.84 us -> none  [body(): terms = lax.all_to_all(terms, 'head', 0, 0, tiled=True)]
    all_to_all x1 -> x0, waiting for transfers between devices: 5.64 us -> none  [body(): terms = lax.all_to_all(terms, 'head', 0, 0, tiled=True)]
    all_to_all x1, blocking collectives: 16.1 us -> 18 us  [body(): lax.all_to_all(parts, 'inst', 0, 0, tiled=True, axis_index_groups=rings)]
    ppermute x1, starting transfers between devices: 0.19 us -> 1.82 us  [body(): first_too = lax.ppermute(first, 'head', pair)]
    ppermute x1, starting transfers between devices: 0.27 us -> 1.88 us  [body(): second = lax.ppermute(second, 'inst', far)]
  transfers between devices with their start and end apart: 7 -> 6, of which waited for: 4 -> 4; matrix products, arithmetic and copies ran while one was open for 0% -> 0% of each run, Pallas kernels for 12% -> 11%
where the time goes in v3:
time: 71.1 us; the launch traced here: 70.8 us
  blocking collectives  28.3 us (40%)
  starting transfers between devices  17.5 us (25%)
  waiting for transfers between devices  11 us (15%)
  Pallas kernels  8.51 us (12%)
  local copies, waits for them, and re-layouts  4.86 us (7%)
    all_to_all x1, blocking collectives, body(): lax.all_to_all(parts, 'inst', 0, 0, tiled=True, axis_index_groups=rings)  18 us
    all_to_all x1, starting transfers between devices, body(): all_queries = lax.all_to_all(copies, 'inst', 0, 0, tiled=True)  11.6 us
    all_to_all x1, blocking collectives, body(): terms = lax.all_to_all(terms, 'head', 0, 0, tiled=True)  10.2 us
    all_to_all x1, waiting for transfers between devices, body(): all_queries = lax.all_to_all(copies, 'inst', 0, 0, tiled=True)  6.36 us
    ppermute x1, waiting for transfers between devices, body(): others = lax.ppermute(parts, 'inst', side)  3.89 us
    unnamed x10, local copies, waits for them, and re-layouts  3.55 us
    pallas_call x1, Pallas kernels, attend(): pl.pallas_call(kernel, out_shape=jax.ShapeDtypeStruct((rows + 8, size), j...  3.4 us
    pallas_call x1, Pallas kernels, gather_pages(): pl.pallas_call(kernel, out_shape=[jax.ShapeDtypeStruct((cut,) + page_pool...  2.75 us
  transfers between devices with their start and end apart: 6, of which 4 were waited for; matrix products, arithmetic and copies ran while one was open for 0% of the time, Pallas kernels for 11%

profile of v3, /device:TPU:1, one launch (start us, length us, event | category | flops | bytes accessed | tf_op | source)
XLA Modules:
  0.0 70.8 jit_solution(6533505805075774424)
XLA Ops:
  0.6 0.0 copy-start.3
  0.6 0.0 copy-start.2
  0.6 1.3 %broadcast_in_dim.8 = bf16[16,8,128]{2,1,0:T(8,128)(2,1)} broadcast(bf16[8,128]{1,0:T(8,128)(2,1)} %bitcast.7), dimensions={1,2} | broadcast | bytes 34816 | tf_op jit(solution)/shard_map/broadcast_in_dim | solution.py:233
  2.0 11.6 %all-to-all-start = ((bf16[16,8,128]{2,1,0:T(8,128)(2,1)}), bf16[16,8,128]{2,1,0:T(8,128)(2,1)S(1)}, u32[]{:S(2)}, u32[]{:S(2)}) async-start(bf16[16,8,128]{2,1,0:T(8,128)(2,1)} %broadcast_in_dim.8), calls=%async_computation | async-start | bytes 65536 | tf_op jit(solution)/shard_map/all_to_all | solution.py:234
  13.5 0.0 copy-start.1
  13.6 2.8 %gather_pages.1 = (bf16[9,2,1,64,128]{4,3,2,1,0:T(8,128)(2,1)}, bf16[7,2,1,64,128]{4,3,2,1,0:T(8,128)(2,1)}) custom-call(s32[1,32]{1,0:T(1,128)} %slots_ref.1, bf16[272,2,1,64,128]{4,3,2,1,0:T(8,128)(2,1)} %pool_ref.3), custom_call_target="tpu_custom_call" | custom-call | tf_op jit(solution)/shard_map/gather_pages/pallas_call | solution.py:31
  16.3 6.4 %all-to-all-done.queries_ref = bf16[16,8,128]{2,1,0:T(8,128)(2,1)S(1)} async-done(((bf16[16,8,128]{2,1,0:T(8,128)(2,1)}), bf16[16,8,128]{2,1,0:T(8,128)(2,1)S(1)}, u32[]{:S(2)}, u32[]{:S(2)}) %all-to-all-start) | async-done | bytes 32800 | tf_op jit(solution)/shard_map/all_to_all | solution.py:234
  22.7 0.6 collective-permute-start
  23.3 0.0 copy-done.3
  23.3 0.0 copy-done.2
  23.3 0.0 copy-start
  23.3 3.5 %copy-done = bf16[272,2,1,64,128]{4,3,2,1,0:T(8,128)(2,1)S(1)} copy-done((bf16[272,2,1,64,128]{4,3,2,1,0:T(8,128)(2,1)S(1)}, bf16[272,2,1,64,128]{4,3,2,1,0:T(8,128)(2,1)}, u32[]{:S(2)}) %copy-start) | copy-done | bytes 8912920
  26.8 0.0 copy-start.4
  26.9 3.4 %attend.1.mine_ref = f32[136,128]{1,0:T(8,128)S(1)} custom-call(s32[16,16]{1,0:T(8,128)S(1)} %bitcast.5, s32[16]{0:T(128)S(1)} %bitcast.6, bf16[16,8,128]{2,1,0:T(8,128)(2,1)S(1)} %all-to-all-done.queries_ref, bf16[272,2,1,64,128]{4,3,2,1,0:T(8,128)(2,1)S(1)} %copy-done), custom_call_target="tpu_custom_call" | custom-call | tf_op jit(solution)/shard_map/attend/pallas_call | solution.py:115
  30.3 1.2 %collective-permute-start.1 = (f32[136,128]{1,0:T(8,128)S(1)}, f32[136,128]{1,0:T(8,128)S(1)}, u32[]{:S(2)}, u32[]{:S(2)}) collective-permute-start(f32[136,128]{1,0:T(8,128)S(1)} %attend.1.mine_ref), channel_id=1, source_target_pairs={{0,16},{16,0},{32,48},{48,32},{64,80},{80,64},{96,112},{112,96},{1... | collective-permute-start | bytes 208904 | tf_op jit(solution)/shard_map/ppermute | solution.py:240
  31.4 3.9 %collective-permute-done.1.theirs_ref = f32[136,128]{1,0:T(8,128)S(1)} collective-permute-done((f32[136,128]{1,0:T(8,128)S(1)}, f32[136,128]{1,0:T(8,128)S(1)}, u32[]{:S(2)}, u32[]{:S(2)}) %collective-permute-start.1) | collective-permute-done | bytes 69664 | tf_op jit(solution)/shard_map/ppermute | solution.py:240
  35.3 0.1 merge_two.1
  35.4 0.2 collective-permute-done.refs_0_
  35.6 18.0 %all_to_all.15.parts_ref = bf16[8,144,128]{2,1,0:T(8,128)(2,1)S(1)} all-to-all(bf16[8,144,128]{2,1,0:T(8,128)(2,1)S(1)} %merge_two.1), channel_id=1, replica_groups={{0,32,64,96,128,160,192,224},{16,48,80,112,144,176,208,240},{1,33,65,97..., dimensions={0} | all-to-all | bytes 589824 | tf_op jit(solution)/shard_map/all_to_all | solution.py:244
  53.7 0.0 copy-done.4
  53.7 1.9 %collective-permute-start.2 = (bf16[7,2,1,64,128]{4,3,2,1,0:T(8,128)(2,1)S(1)}, bf16[7,2,1,64,128]{4,3,2,1,0:T(8,128)(2,1)S(1)}, u32[]{:S(2)}, u32[]{:S(2)}) collective-permute-start(bf16[7,2,1,64,128]{4,3,2,1,0:T(8,128)(2,1)S(1)} %copy-done.4), channel_id=1, source_target_pairs={{0,128},{16,144},{32,160},{48,176},{64,192},{80,208},{96,224},{112... | collective-permute-start | bytes 688136 | tf_op jit(solution)/shard_map/ppermute | solution.py:247
  55.5 1.8 %collective-permute-start.3 = (bf16[9,2,1,64,128]{4,3,2,1,0:T(8,128)(2,1)S(1)}, bf16[9,2,1,64,128]{4,3,2,1,0:T(8,128)(2,1)S(1)}, u32[]{:S(2)}, u32[]{:S(2)}) collective-permute-start(bf16[9,2,1,64,128]{4,3,2,1,0:T(8,128)(2,1)S(1)} %collective-permute-done.refs_0_), channel_id=1, source_target_pairs={{0,1},{1,0},{2,3},{3,2},{4,5},{5,4},{6,7},{7,6},{8,9},{9,8},{10,11... | collective-permute-start | bytes 884744 | tf_op jit(solution)/shard_map/ppermute | solution.py:243
  57.4 0.0 copy-done.1
  57.4 0.6 combine_and_project.1
  58.0 10.2 %all_to_all.16.terms_ref = f32[16,8,128]{2,1,0:T(8,128)S(1)} all-to-all(f32[16,8,128]{2,1,0:T(8,128)S(1)} %bitcast.4), channel_id=1, replica_groups=mesh['inst'=16,'head'=16] {'head'}, dimensions={0} | all-to-all | bytes 131072 | tf_op jit(solution)/shard_map/all_to_all | solution.py:250
  68.3 0.0 collective-permute-done.2.refs_1_
  68.3 0.4 collective-permute-start.4
  68.7 0.6 sum_terms.1
  69.3 0.0 collective-permute-done.3.refs_2_
  69.3 0.5 collective-permute-done.4.refs_3_
  69.8 1.0 %join_pieces.1 = bf16[32,2,1,64,128]{4,3,2,1,0:T(8,128)(2,1)} custom-call(bf16[9,2,1,64,128]{4,3,2,1,0:T(8,128)(2,1)S(1)} %collective-permute-done.refs_0_, bf16[7,2,1,64,128]{4,3,2,1,0:T(8,128)(2,1)S(1)} %collective-permute-done.2.refs_1_, bf16[9,2,1,64,128]{4,3,2,1,0:T(8,128)(2,1)S(1)} %collective-permute-done.3.refs_2_, ...), custom_call_target="tpu_custom_call" | custom-call | tf_op jit(solution)/shard_map/join_pieces/pallas_call | solution.py:67
Async XLA Ops:
  0.6 22.7 %copy-start.3 = (s32[16,1]{0,1:T(1,128)S(1)}, s32[16,1]{0,1:T(1,128)}, u32[]{:S(2)}) copy-start(s32[16,1]{0,1:T(1,128)} %param.9) | copy-start | bytes 196
  0.6 22.7 %copy-start.2 = (s32[16,1,16]{2,1,0:T(1,128)S(1)}, s32[16,1,16]{2,1,0:T(1,128)}, u32[]{:S(2)}) copy-start(s32[16,1,16]{2,1,0:T(1,128)} %param.8) | copy-start | bytes 3076
  2.0 20.7 %all-to-all-start = ((bf16[16,8,128]{2,1,0:T(8,128)(2,1)}), bf16[16,8,128]{2,1,0:T(8,128)(2,1)S(1)}, u32[]{:S(2)}, u32[]{:S(2)}) async-start(bf16[16,8,128]{2,1,0:T(8,128)(2,1)} %broadcast_in_dim.8), calls=%async_computation | async-start | bytes 65536 | tf_op jit(solution)/shard_map/all_to_all | solution.py:234
  13.5 43.8 %copy-start.1 = (bf16[1024,1024]{1,0:T(8,128)(2,1)S(1)}, bf16[1024,1024]{1,0:T(8,128)(2,1)}, u32[]{:S(2)}) copy-start(bf16[1024,1024]{1,0:T(8,128)(2,1)} %weight_ref.1) | copy-start | bytes 6291460
  22.7 13.0 %collective-permute-start = (bf16[9,2,1,64,128]{4,3,2,1,0:T(8,128)(2,1)}, bf16[9,2,1,64,128]{4,3,2,1,0:T(8,128)(2,1)S(1)}, u32[]{:S(2)}, u32[]{:S(2)}) collective-permute-start(bf16[9,2,1,64,128]{4,3,2,1,0:T(8,128)(2,1)} %get-tuple-element.14), channel_id=1, source_target_pairs={{0,128},{16,144},{32,160},{48,176},{64,192},{80,208},{96,224},{112... | collective-permute-start | bytes 884744 | tf_op jit(solution)/shard_map/ppermute | solution.py:238
  23.3 3.5 %copy-start = (bf16[272,2,1,64,128]{4,3,2,1,0:T(8,128)(2,1)S(1)}, bf16[272,2,1,64,128]{4,3,2,1,0:T(8,128)(2,1)}, u32[]{:S(2)}) copy-start(bf16[272,2,1,64,128]{4,3,2,1,0:T(8,128)(2,1)} %pool_ref.3) | copy-start | bytes 26738692
  26.8 26.8 %copy-start.4 = (bf16[7,2,1,64,128]{4,3,2,1,0:T(8,128)(2,1)S(1)}, bf16[7,2,1,64,128]{4,3,2,1,0:T(8,128)(2,1)}, u32[]{:S(2)}) copy-start(bf16[7,2,1,64,128]{4,3,2,1,0:T(8,128)(2,1)} %get-tuple-element.17) | copy-start | bytes 688132
  30.3 5.0 %collective-permute-start.1 = (f32[136,128]{1,0:T(8,128)S(1)}, f32[136,128]{1,0:T(8,128)S(1)}, u32[]{:S(2)}, u32[]{:S(2)}) collective-permute-start(f32[136,128]{1,0:T(8,128)S(1)} %attend.1.mine_ref), channel_id=1, source_target_pairs={{0,16},{16,0},{32,48},{48,32},{64,80},{80,64},{96,112},{112,96},{1... | collective-permute-start | bytes 208904 | tf_op jit(solution)/shard_map/ppermute | solution.py:240
  53.7 14.6 %collective-permute-start.2 = (bf16[7,2,1,64,128]{4,3,2,1,0:T(8,128)(2,1)S(1)}, bf16[7,2,1,64,128]{4,3,2,1,0:T(8,128)(2,1)S(1)}, u32[]{:S(2)}, u32[]{:S(2)}) collective-permute-start(bf16[7,2,1,64,128]{4,3,2,1,0:T(8,128)(2,1)S(1)} %copy-done.4), channel_id=1, source_target_pairs={{0,128},{16,144},{32,160},{48,176},{64,192},{80,208},{96,224},{112... | collective-permute-start | bytes 688136 | tf_op jit(solution)/shard_map/ppermute | solution.py:247
  55.5 13.8 %collective-permute-start.3 = (bf16[9,2,1,64,128]{4,3,2,1,0:T(8,128)(2,1)S(1)}, bf16[9,2,1,64,128]{4,3,2,1,0:T(8,128)(2,1)S(1)}, u32[]{:S(2)}, u32[]{:S(2)}) collective-permute-start(bf16[9,2,1,64,128]{4,3,2,1,0:T(8,128)(2,1)S(1)} %collective-permute-done.refs_0_), channel_id=1, source_target_pairs={{0,1},{1,0},{2,3},{3,2},{4,5},{5,4},{6,7},{7,6},{8,9},{9,8},{10,11... | collective-permute-start | bytes 884744 | tf_op jit(solution)/shard_map/ppermute | solution.py:243
  68.3 1.6 %collective-permute-start.4 = (bf16[7,2,1,64,128]{4,3,2,1,0:T(8,128)(2,1)S(1)}, bf16[7,2,1,64,128]{4,3,2,1,0:T(8,128)(2,1)S(1)}, u32[]{:S(2)}, u32[]{:S(2)}) collective-permute-start(bf16[7,2,1,64,128]{4,3,2,1,0:T(8,128)(2,1)S(1)} %collective-permute-done.2.refs_1_), channel_id=1, source_target_pairs={{0,1},{1,0},{2,3},{3,2},{4,5},{5,4},{6,7},{7,6},{8,9},{9,8},{10,11... | collective-permute-start | bytes 688136 | tf_op jit(solution)/shard_map/ppermute | solution.py:252
